TPU v7x, 32 devices: a whole 2x2x4 slice. The times are simulated.
32 devices in a mesh: groups: 2 (over y), tm: 4 (over z), sensor: 2 (over x), state: 2 (over core).
Axes of the slice: x: 2, y: 2, z: 4, core: 2. Of those that a mesh axis runs over, the one named last changes fastest.
Arguments:
- obs_rows: bfloat16 [64, 2048, 256], P('groups', ('tm', 'sensor', 'state')), parts along dimension 0, may hold values from -0.375 to 0.375
- readings: float32 [64, 2048], P('groups', ('tm', 'sensor', 'state')), parts along dimension 0, may hold values from -6 to 6
- available: int32 [64, 2048], P('groups', ('tm', 'sensor', 'state')), parts along dimension 0, may hold values 0 or 1
- sensor_ids: int32 [4096], P(('groups', 'tm', 'sensor', 'state')), parts along dimension 0, may hold values from 0 to 2047, each once
- noise_var: float32 [2048], replicated, may hold values from 0.5 to 4
- col_scale: float32 [256], replicated, may hold values from 0.05 to 1
- transition: float32 [256, 256], replicated, may hold values from -0.0025 to 1
- process_info: float32 [256, 256], replicated, may hold values from -3.125 to 1000, as said below
Outputs:
- filtered_mean: float32 [64, 256], P(('groups', 'tm', 'sensor', 'state')), parts along dimension 0
- filtered_cov: float32 [64, 256, 256], P(('groups', 'tm', 'sensor', 'state')), parts along dimension 0
There are 2 independent parts, one for each index of `groups`. A program takes and returns all parts, laid end to end along the dimension named above; an argument that names none is the same for every part. Nothing has to cross between parts.
Inputs may be any that keep to these rules, and one draw needn't show every extreme that they name: `sensor_ids`: each stored column holds a different sensor. `process_info`: symmetric positive definite.
All inputs are finite; a program needn't handle non-finite values. No bound on the sum of `available` on one device may be relied on, other than what follows from the above.
Results may differ from a plain program's by a relative error of at most 0.0043.
Values may be sent and summed in bfloat16 or wider, within the bound.
A program may use at most 128 MiB of HBM per device.

v0:
```python
import jax
import jax.numpy as jnp
from jax import lax
from jax.sharding import PartitionSpec as P

highest = lax.Precision.HIGHEST


def prefix(x, axis, combine, identity):
    peers, mine = (lax.axis_size(axis), lax.axis_index(axis))
    everything = jax.tree.map(lambda part: lax.all_gather(part, axis), x)
    start = jax.tree.map(
        lambda part, zero: jnp.broadcast_to(jnp.asarray(zero, part.dtype), part.shape), x, identity
    )

    def hop(k, before):
        reached = k < mine
        new = combine(before, jax.tree.map(lambda part: part[k], everything))
        return jax.tree.map(lambda a, b: jnp.where(reached, a, b), new, before)

    return lax.fori_loop(0, peers, hop, start)


def from_root(x, axis, root):
    mine = lax.axis_index(axis) == root
    return lax.psum(jnp.where(mine, x, jnp.zeros_like(x)), axis)


def matmul(first_op, second_op):
    return jnp.dot(first_op, second_op, precision=highest)


def invert_shifted(matrix):
    factor = jnp.linalg.cholesky(matmul(matrix.T, matrix))
    return jax.scipy.linalg.cho_solve((factor, True), matrix.T)


def build_element(gram_part, info_part, col_scale, transition, process_info, carried, keep_flag):
    state_dim = gram_part.shape[0]
    information = gram_part * (col_scale[:, None] * col_scale[None, :])
    vector = info_part * col_scale
    factor = jnp.linalg.cholesky(process_info + information)
    spread = jax.scipy.linalg.cho_solve((factor, True), jnp.eye(state_dim, dtype=jnp.float32))
    offset = matmul(spread, vector)
    forward = matmul(spread, carried) * keep_flag
    residual = vector - matmul(information, offset)
    backward = matmul(residual, transition) * keep_flag
    inner_term = information - matmul(matmul(information, spread), information)
    precision_part = matmul(matmul(transition.T, inner_term), transition) * keep_flag
    return (forward, offset, spread, backward, precision_part)


def combine(earlier, later):
    first_a, first_b, first_c, first_e, first_j = earlier
    later_a, later_b, later_c, later_e, later_j = later
    state_dim = first_a.shape[0]
    shifted = jnp.eye(state_dim, dtype=jnp.float32) + matmul(first_c, later_j)
    inverse = invert_shifted(shifted)
    mixing = matmul(later_a, inverse)
    back_mix = matmul(first_a.T, inverse.T)
    new_a = matmul(mixing, first_a)
    new_b = matmul(mixing, first_b + matmul(first_c, later_e)) + later_b
    new_c = matmul(matmul(mixing, first_c), later_a.T) + later_c
    new_e = matmul(back_mix, later_e - matmul(later_j, first_b)) + first_e
    new_j = matmul(matmul(back_mix, later_j), first_a) + first_j
    return (new_a, new_b, new_c, new_e, new_j)


def advance(running, element):
    prior_mean, prior_cov = running
    later_a, later_b, later_c, later_e, later_j = element
    state_dim = prior_cov.shape[0]
    shifted = jnp.eye(state_dim, dtype=jnp.float32) + matmul(prior_cov, later_j)
    mixing = matmul(later_a, invert_shifted(shifted))
    new_mean = matmul(mixing, prior_mean + matmul(prior_cov, later_e)) + later_b
    new_cov = matmul(matmul(mixing, prior_cov), later_a.T) + later_c
    return (new_mean, new_cov)


def select_element(elements, counter):
    return tuple((member[counter] for member in elements))


def pack_element(element):
    state_dim = element[0].shape[0]
    filler = jnp.zeros((6, state_dim), jnp.float32)
    return jnp.concatenate(
        [element[0], element[2], element[4], element[1][None, :], element[3][None, :], filler],
        axis=0,
    )


def unpack_element(packed):
    state_dim = packed.shape[1]
    first_a = packed[0:state_dim]
    first_c = packed[state_dim : 2 * state_dim]
    first_j = packed[2 * state_dim : 3 * state_dim]
    first_b = packed[3 * state_dim]
    first_e = packed[3 * state_dim + 1]
    return (first_a, first_b, first_c, first_e, first_j)


def gram_terms(weighted, signal):
    gram_part = jnp.einsum("tms,tmu->tsu", weighted, weighted, preferred_element_type=jnp.float32)
    info_part = jnp.einsum("tm,tms->ts", signal, weighted, preferred_element_type=jnp.float32)
    return (gram_part, info_part)


def body(obs_rows, readings, available, sensor_ids, noise_var, col_scale, transition, process_info):
    state_dim = obs_rows.shape[2]
    sensor_total = noise_var.shape[0]
    lookup_table = (
        sensor_ids[:, None] == jnp.arange(sensor_total, dtype=jnp.int32)[None, :]
    ).astype(jnp.float32)
    local_var = matmul(lookup_table, noise_var)
    weight = available.astype(jnp.float32) * lax.rsqrt(local_var)[None, :]
    weighted = (obs_rows.astype(jnp.float32) * weight[:, :, None]).astype(jnp.bfloat16)
    signal = (readings * weight).astype(jnp.bfloat16)
    arrived = (
        lax.all_to_all(weighted, "tm", split_axis=0, concat_axis=1, tiled=True),
        lax.all_to_all(signal, "tm", split_axis=0, concat_axis=1, tiled=True),
    )
    gram_part, info_part = gram_terms(arrived[0], arrived[1])
    gram_part, info_part = (
        lax.psum_scatter(gram_part, ("sensor", "state"), scatter_dimension=0, tiled=True),
        lax.psum_scatter(info_part, ("sensor", "state"), scatter_dimension=0, tiled=True),
    )
    block_len = gram_part.shape[0]
    position = lax.axis_index(("tm", "sensor", "state")) * block_len + jnp.arange(
        block_len, dtype=jnp.int32
    )
    keep_flag = (position > 0).astype(jnp.float32)
    carried = matmul(process_info, transition)
    elements = jax.vmap(build_element, in_axes=(0, 0, None, None, None, None, 0))(
        gram_part, info_part, col_scale, transition, process_info, carried, keep_flag
    )
    summary = select_element(elements, 0)
    counter = 1
    summary = combine(summary, select_element(elements, counter))
    zero_vec = jnp.zeros((state_dim,), jnp.float32)
    zero_mat = jnp.zeros((state_dim, state_dim), jnp.float32)
    identity_el = (jnp.eye(state_dim, dtype=jnp.float32), zero_vec, zero_mat, zero_vec, zero_mat)
    inner_prefix = prefix(summary, ("sensor", "state"), combine, identity_el)
    through = combine(inner_prefix, summary)
    group_last = lax.axis_size(("sensor", "state")) - 1
    totals = unpack_element(from_root(pack_element(through), ("sensor", "state"), group_last))
    outer_prefix = prefix(totals, "tm", combine, identity_el)
    incoming = combine(outer_prefix, inner_prefix)
    running = (incoming[1], incoming[2])
    mean_list = []
    cov_list = []
    for counter in range(block_len):
        running = advance(running, select_element(elements, counter))
        mean_list.append(running[0])
        cov_list.append(running[1])
    return (jnp.stack(mean_list), jnp.stack(cov_list))


def solution(mesh):
    in_specs = (
        P("groups", ("tm", "sensor", "state"), None),
        P("groups", ("tm", "sensor", "state")),
        P("groups", ("tm", "sensor", "state")),
        P(("groups", "tm", "sensor", "state")),
        P(),
        P(),
        P(),
        P(),
    )
    out_specs = (
        P(("groups", "tm", "sensor", "state"), None),
        P(("groups", "tm", "sensor", "state"), None, None),
    )
    return jax.shard_map(body, mesh=mesh, in_specs=in_specs, out_specs=out_specs, check_vma=False)
```

profile of v0, /device:TPU:29, one launch (start us, length us, event | category | flops | bytes accessed | tf_op | source)
XLA Modules:
  0.0 1337.2 jit_solution(8376007178597351594)
XLA Ops:
  11.9 50.4 %all_to_all.37 = bf16[32,128,256]{2,1,0:T(8,128)(2,1)S(1)} all-to-all(bf16[32,128,256]{2,1,0:T(8,128)(2,1)S(1)} %multiply_convert_fusion), channel_id=1, replica_groups=mesh['groups'=2,'tm'=4,'sensor'=2,'state'=2] {'tm'}, dimensions={0} | all-to-all | bytes 4194304 | tf_op jit(solution)/shard_map/all_to_all | solution.py:120
  70.7 26.8 %reduce-scatter.2.cloned.1.call-done = f32[2,256,256]{1,2,0:T(8,128)} async-done(((f32[8,256,256]{1,2,0:T(8,128)}), f32[2,256,256]{1,2,0:T(8,128)}) %reduce-scatter.2.cloned.1.call-update) | async-done | bytes 524304 | tf_op jit(solution)/shard_map/reduce_scatter | solution.py:125
  103.6 23.5 %custom-call.33 = f32[2,128,128]{2,1,0:T(8,128)S(1)} custom-call(f32[2,128,128]{2,1,0:T(8,128)S(1)} %cholesky.702), custom_call_target="Cholesky" | custom-call | tf_op jit(solution)/shard_map/vmap(jit(cholesky))/cholesky | solution.py:42
  128.5 21.1 %custom-call.34 = f32[2,1,128,128]{2,3,1,0:T(8,128)} custom-call(f32[2,1,128,128]{3,2,1,0:T(8,128)} %select_bitcast_fusion.2), custom_call_target="InvertDiagBlocksLowerTriangular" | custom-call | tf_op jit(solution)/shard_map/vmap(jit(cholesky))/cholesky | solution.py:42
  152.8 24.9 %custom-call.35 = f32[2,128,128]{2,1,0:T(8,128)} custom-call(f32[2,128,128]{2,1,0:T(8,128)} %convolution_subtract_fusion.19), custom_call_target="Cholesky" | custom-call | tf_op jit(solution)/shard_map/vmap(jit(cholesky))/cholesky | solution.py:42
  186.6 41.0 %custom-call.36 = f32[2,2,128,128]{2,3,1,0:T(8,128)} custom-call(f32[2,2,128,128]{3,2,1,0:T(8,128)} %bitcast.804), custom_call_target="InvertDiagBlocksLowerTriangular" | custom-call | tf_op jit(solution)/shard_map/vmap(jit(_cho_solve))/triangular_solve | solution.py:43
  256.4 19.9 %custom-call.59 = f32[1,128,128]{1,2,0:T(8,128)S(1)} custom-call(f32[1,128,128]{2,1,0:T(8,128)S(1)} %get-tuple-element.676), custom_call_target="InvertDiagBlocksLowerTriangular" | custom-call | tf_op jit(solution)/shard_map/jit(cholesky)/cholesky | solution.py:34
  278.4 11.7 cholesky.547
  299.6 20.5 %custom-call.60 = f32[2,128,128]{1,2,0:T(8,128)S(1)} custom-call(f32[2,128,128]{2,1,0:T(8,128)} %copy-done.30), custom_call_target="InvertDiagBlocksLowerTriangular" | custom-call | tf_op jit(solution)/shard_map/jit(_cho_solve)/triangular_solve | solution.py:35
  368.5 17.2 %all-gather.19.cloned.1.call-done = f32[1024,256]{1,0:T(8,128)} async-done(((f32[256,256]{1,0:T(8,128)}), f32[1024,256]{1,0:T(8,128)}) %all-gather.19.cloned.1.call-update) | async-done | bytes 1048592 | tf_op jit(solution)/shard_map/all_gather | solution.py:11
  385.7 281.8 %while.57 = (s32[]{:T(128)}, f32[256,256]{1,0:T(8,128)S(1)}, f32[256]{0:T(256)S(1)}, f32[256,256]{1,0:T(8,128)S(1)}, f32[256]{0:T(256)S(1)}, /*index=5*/f32[256,...) while((s32[]{:T(128)}, f32[256,256]{1,0:T(8,128)S(1)}, ...), condition=%wide.region_11.14_spmd.clone, body=%wide.region_10.13_spmd.clone.sunk | while | flops 2169194752 | bytes 19102112 | solution.py:21
  388.3 11.7 cholesky.1131
  410.4 11.7 cholesky.1133
  428.5 19.7 %custom-call.80 = f32[2,128,128]{1,2,0:T(8,128)S(1)} custom-call(f32[2,128,128]{2,1,0:T(8,128)S(1)} %get-tuple-element.1068), custom_call_target="InvertDiagBlocksLowerTriangular" | custom-call | tf_op jit(solution)/shard_map/while/body/eval_jaxpr/jit(_cho_solve)/triangular_solve | solution.py:35
  458.6 11.7 cholesky.1131
  480.7 11.7 cholesky.1133
  498.8 19.7 %custom-call.80 = f32[2,128,128]{1,2,0:T(8,128)S(1)} custom-call(f32[2,128,128]{2,1,0:T(8,128)S(1)} %get-tuple-element.1068), custom_call_target="InvertDiagBlocksLowerTriangular" | custom-call | tf_op jit(solution)/shard_map/while/body/eval_jaxpr/jit(_cho_solve)/triangular_solve | solution.py:35
  528.9 11.7 cholesky.1131
  551.0 11.7 cholesky.1133
  569.2 19.7 %custom-call.80 = f32[2,128,128]{1,2,0:T(8,128)S(1)} custom-call(f32[2,128,128]{2,1,0:T(8,128)S(1)} %get-tuple-element.1068), custom_call_target="InvertDiagBlocksLowerTriangular" | custom-call | tf_op jit(solution)/shard_map/while/body/eval_jaxpr/jit(_cho_solve)/triangular_solve | solution.py:35
  599.3 11.7 cholesky.1131
  621.3 11.7 cholesky.1133
  639.5 19.7 %custom-call.80 = f32[2,128,128]{1,2,0:T(8,128)S(1)} custom-call(f32[2,128,128]{2,1,0:T(8,128)S(1)} %get-tuple-element.1068), custom_call_target="InvertDiagBlocksLowerTriangular" | custom-call | tf_op jit(solution)/shard_map/while/body/eval_jaxpr/jit(_cho_solve)/triangular_solve | solution.py:35
  669.7 11.7 cholesky.564
  691.8 11.7 cholesky.581
  710.2 19.9 %custom-call.62 = f32[2,128,128]{1,2,0:T(8,128)S(1)} custom-call(f32[2,128,128]{2,1,0:T(8,128)S(1)} %get-tuple-element.493), custom_call_target="InvertDiagBlocksLowerTriangular" | custom-call | tf_op jit(solution)/shard_map/jit(_cho_solve)/triangular_solve | solution.py:35
  737.4 33.6 %all-reduce.5.cloned.1.call-done = f32[776,256]{1,0:T(8,128)} async-done(((f32[776,256]{1,0:T(8,128)}), f32[776,256]{1,0:T(8,128)}) %all-reduce.5.cloned.1.call-update) | async-done | bytes 794640 | tf_op jit(solution)/shard_map/psum | solution.py:26
  789.4 11.8 all-gather.25.cloned.1.call-done
  801.2 29.1 %all-gather.27.cloned.1.call-done = f32[1024,256]{1,0:T(8,128)} async-done(((f32[256,256]{1,0:T(8,128)}), f32[1024,256]{1,0:T(8,128)}) %all-gather.27.cloned.1.call-update) | async-done | bytes 1048592 | tf_op jit(solution)/shard_map/all_gather | solution.py:11
  830.3 29.1 %all-gather.29.cloned.1.call-done = f32[1024,256]{1,0:T(8,128)} async-done(((f32[256,256]{1,0:T(8,128)}), f32[1024,256]{1,0:T(8,128)}) %all-gather.29.cloned.1.call-update) | async-done | bytes 1048592 | tf_op jit(solution)/shard_map/all_gather | solution.py:11
  859.4 271.0 %while.59 = (s32[]{:T(128)}, f32[256]{0:T(256)S(1)}, f32[256,256]{1,0:T(8,128)S(1)}, s32[]{:T(128)}, f32[4,256,256]{2,1,0:T(8,128)}, /*index=5*/f32[4,256,256]{2...) while((s32[]{:T(128)}, f32[256]{0:T(256)S(1)}, ...), condition=%wide.region_14.17_spmd.clone, body=%wide.region_13.16_spmd.clone.sunk | while | flops 1361987072 | bytes 10437990 | solution.py:21
  862.0 11.7 cholesky.1157
  884.1 11.7 cholesky.1159
  902.1 19.7 %custom-call.83 = f32[2,128,128]{1,2,0:T(8,128)S(1)} custom-call(f32[2,128,128]{2,1,0:T(8,128)S(1)} %get-tuple-element.1093), custom_call_target="InvertDiagBlocksLowerTriangular" | custom-call | tf_op jit(solution)/shard_map/while/body/eval_jaxpr/jit(_cho_solve)/triangular_solve | solution.py:35
  929.6 11.7 cholesky.1157
  951.7 11.7 cholesky.1159
  969.6 19.7 %custom-call.83 = f32[2,128,128]{1,2,0:T(8,128)S(1)} custom-call(f32[2,128,128]{2,1,0:T(8,128)S(1)} %get-tuple-element.1093), custom_call_target="InvertDiagBlocksLowerTriangular" | custom-call | tf_op jit(solution)/shard_map/while/body/eval_jaxpr/jit(_cho_solve)/triangular_solve | solution.py:35
  997.2 11.7 cholesky.1157
  1019.3 11.7 cholesky.1159
  1037.2 19.7 %custom-call.83 = f32[2,128,128]{1,2,0:T(8,128)S(1)} custom-call(f32[2,128,128]{2,1,0:T(8,128)S(1)} %get-tuple-element.1093), custom_call_target="InvertDiagBlocksLowerTriangular" | custom-call | tf_op jit(solution)/shard_map/while/body/eval_jaxpr/jit(_cho_solve)/triangular_solve | solution.py:35
  1086.9 11.7 cholesky.1159
  1104.8 19.7 %custom-call.83 = f32[2,128,128]{1,2,0:T(8,128)S(1)} custom-call(f32[2,128,128]{2,1,0:T(8,128)S(1)} %get-tuple-element.1093), custom_call_target="InvertDiagBlocksLowerTriangular" | custom-call | tf_op jit(solution)/shard_map/while/body/eval_jaxpr/jit(_cho_solve)/triangular_solve | solution.py:35
  1153.6 11.7 cholesky.615
  1172.2 20.1 %custom-call.64 = f32[2,128,128]{1,2,0:T(8,128)S(1)} custom-call(f32[2,128,128]{2,1,0:T(8,128)S(1)} %get-tuple-element.494), custom_call_target="InvertDiagBlocksLowerTriangular" | custom-call | tf_op jit(solution)/shard_map/jit(_cho_solve)/triangular_solve | solution.py:35
  1219.9 11.9 cholesky.649
  1238.6 19.7 %custom-call.66 = f32[2,128,128]{1,2,0:T(8,128)S(1)} custom-call(f32[2,128,128]{2,1,0:T(8,128)S(1)} %get-tuple-element.495), custom_call_target="InvertDiagBlocksLowerTriangular" | custom-call | tf_op jit(solution)/shard_map/jit(_cho_solve)/triangular_solve | solution.py:35
  1285.9 11.9 cholesky.683
  1304.5 19.7 %custom-call.68 = f32[2,128,128]{1,2,0:T(8,128)S(1)} custom-call(f32[2,128,128]{2,1,0:T(8,128)S(1)} %get-tuple-element.496), custom_call_target="InvertDiagBlocksLowerTriangular" | custom-call | tf_op jit(solution)/shard_map/jit(_cho_solve)/triangular_solve | solution.py:35
  (701 shorter events, 528.3 us)
Async XLA Ops:
  7.2 61.6 %copy-start = (f32[256,256]{1,0:T(8,128)S(1)}, f32[256,256]{1,0:T(8,128)}, u32[]{:S(2)}) copy-start(f32[256,256]{1,0:T(8,128)} %param.21) | copy-start | bytes 786436
  7.2 90.4 %reduce-scatter.2.cloned.1.call-start = ((), (), s32[]{:S(2)}) async-start(), calls=%async_computation.3 | async-start | bytes 2621440 | tf_op jit(solution)/shard_map/reduce_scatter | solution.py:125
  64.5 0.9 copy-start.25
  64.5 5.3 copy-start.31
  64.6 303.9 %all-gather.23.cloned.1.call-start = ((), (), s32[]{:S(2)}) async-start(), calls=%async_computation.7 | async-start | bytes 1310720 | tf_op jit(solution)/shard_map/all_gather | solution.py:11
  70.0 165.0 %copy-start.8 = (f32[256,256]{0,1:T(8,128)}, f32[256,256]{0,1:T(8,128)S(1)}, u32[]{:S(2)}) copy-start(f32[256,256]{0,1:T(8,128)S(1)} %broadcast_multiply_fusion) | copy-start | bytes 786436
  97.5 4.1 copy-start.5
  102.8 0.8 copy-start.22
  178.7 0.8 copy-start.21
  178.7 50.3 %copy-start.29 = (f32[128,256]{1,0:T(8,128)S(1)}, f32[128,256]{1,0:T(8,128)}, u32[]{:S(2)}) copy-start(f32[128,256]{1,0:T(8,128)} %get-tuple-element.654) | copy-start | bytes 393220
  186.6 42.8 %copy-start.17 = (f32[2,256,256]{2,1,0:T(8,128)}, f32[2,256,256]{2,1,0:T(8,128)S(1)}, u32[]{:S(2)}) copy-start(f32[2,256,256]{2,1,0:T(8,128)S(1)} %get-tuple-element.1364) | copy-start | bytes 1572868
  227.6 5.9 copy-start.26
  229.0 4.9 copy-start.6
  232.0 118.7 %copy-start.1 = (f32[2,128,256]{2,1,0:T(8,128)}, f32[2,128,256]{2,1,0:T(8,128)S(1)}, u32[]{:S(2)}) copy-start(f32[2,128,256]{2,1,0:T(8,128)S(1)} %fusion.169) | copy-start | bytes 786436
  233.9 5.6 copy-start.9
  233.9 2.4 copy-start.24
  233.9 2.4 copy-start.33
  243.9 0.7 copy-start.27
  293.4 35.8 %copy-start.10 = (f32[256,256]{1,0:T(8,128)S(1)}, f32[256,256]{1,0:T(8,128)}, u32[]{:S(2)}) copy-start(f32[256,256]{1,0:T(8,128)} %copy-done.9) | copy-start | bytes 786436
  299.0 0.7 copy-start.30
  320.1 2.6 copy-start.28
  326.5 0.7 copy-start.23
  328.5 0.7 copy-start.14
  329.6 12.0 copy-start.34
  331.7 36.8 %all-gather.21.cloned.1.call-start = ((), (), s32[]{:S(2)}) async-start(), calls=%async_computation.6 | async-start | bytes 1310720 | tf_op jit(solution)/shard_map/all_gather | solution.py:11
  333.3 8.2 copy-start.18
  333.3 17.4 %copy-start.32 = (f32[256]{0:T(256)S(1)}, f32[256]{0:T(256)}, u32[]{:S(2)}) copy-start(f32[256]{0:T(256)} %param.20) | copy-start | bytes 3076
  336.9 6.4 all-to-all-start.1
  341.5 44.3 %all-gather.19.cloned.1.call-start = ((), (), s32[]{:S(2)}) async-start(), calls=%async_computation.5 | async-start | bytes 1310720 | tf_op jit(solution)/shard_map/all_gather | solution.py:11
  343.7 11.5 copy-start.11
  343.7 11.9 copy-start.15
  343.7 19.4 %copy-start.19 = (f32[256,256]{1,0:T(8,128)S(1)}, f32[256,256]{1,0:T(8,128)}, u32[]{:S(2)}) copy-start(f32[256,256]{1,0:T(8,128)} %copy-done.18) | copy-start | bytes 786436
  343.7 42.0 %copy-start.7 = (f32[256,256]{1,0:T(8,128)S(1)}, f32[256,256]{1,0:T(8,128)}, u32[]{:S(2)}) copy-start(f32[256,256]{1,0:T(8,128)} %custom-call.52) | copy-start | bytes 786436
  353.5 417.6 %all-reduce.5.cloned.1.call-start = ((), (), s32[]{:S(2)}) async-start(), calls=%async_computation.4 | async-start | bytes 1589248 | tf_op jit(solution)/shard_map/psum | solution.py:26
  450.0 4.1 copy-start.4
  520.3 4.1 copy-start.4
  590.6 4.1 copy-start.4
  660.9 4.1 copy-start.4
  691.5 40.4 %copy-start.16 = (f32[256,256]{1,0:T(8,128)S(1)}, f32[256,256]{1,0:T(8,128)}, u32[]{:S(2)}) copy-start(f32[256,256]{1,0:T(8,128)} %fusion.152) | copy-start | bytes 786436
  731.1 2.6 copy-start.13
  732.4 3.1 copy-start.20
  737.4 63.8 %all-gather.25.cloned.1.call-start = ((), (), s32[]{:S(2)}) async-start(), calls=%async_computation.8 | async-start | bytes 1310720 | tf_op jit(solution)/shard_map/all_gather | solution.py:11
  773.1 57.2 %all-gather.27.cloned.1.call-start = ((), (), s32[]{:S(2)}) async-start(), calls=%async_computation.9 | async-start | bytes 1310720 | tf_op jit(solution)/shard_map/all_gather | solution.py:11
  773.9 85.5 %all-gather.29.cloned.1.call-start = ((), (), s32[]{:S(2)}) async-start(), calls=%async_computation.10 | async-start | bytes 1310720 | tf_op jit(solution)/shard_map/all_gather | solution.py:11
  1219.6 40.5 %copy-start.3 = (f32[2,256,256]{2,1,0:T(8,128)S(1)}, f32[2,256,256]{2,1,0:T(8,128)}, u32[]{:S(2)}) copy-start(f32[2,256,256]{2,1,0:T(8,128)} %convolution_multiply_fusion.1) | copy-start | bytes 1572868
  1238.5 22.4 %copy-start.12 = (f32[256,256]{1,0:T(8,128)S(1)}, f32[256,256]{1,0:T(8,128)}, u32[]{:S(2)}) copy-start(f32[256,256]{1,0:T(8,128)} %copy-done.9) | copy-start | bytes 786436
  1304.5 22.4 %copy-start.2 = (f32[2,128,256]{2,1,0:T(8,128)S(1)}, f32[2,128,256]{2,1,0:T(8,128)}, u32[]{:S(2)}) copy-start(f32[2,128,256]{2,1,0:T(8,128)} %copy-done.1) | copy-start | bytes 786436
Sparse Core Ops, SparseCore 0:
  64.7 32.8 reduce-scatter.1
  331.8 17.1 all-gather.22
  350.6 16.7 all-gather.20
  368.9 16.8 all-gather.18
  737.5 33.5 all-reduce.4
  773.2 27.9 all-gather.24
  802.9 27.4 all-gather.26
  832.0 27.4 all-gather.28
where the time goes:
time: 1350 us; the launch traced here: 1340 us
  other arithmetic  842 us (62%)
  waiting for transfers between devices  150 us (11%)
  matrix products  145 us (11%)
  blocking collectives  82.3 us (6%)
  local copies, waits for them, and re-layouts  76.5 us (6%)
  between operations  22.9 us (2%)
  loops' own time  14.2 us (1%)
    another operation x83, other arithmetic, invert_shifted(): factor = jnp.linalg.cholesky(matmul(matrix.T, matrix))  456 us
    another operation x42, other arithmetic, invert_shifted(): return jax.scipy.linalg.cho_solve((factor, True), matrix.T)  258 us
    dot_general x137, matrix products, matmul(): return jnp.dot(first_op, second_op, precision=highest)  98.1 us
    all_gather x6, waiting for transfers between devices, prefix(): everything = jax.tree.map(lambda part: lax.all_gather(part, axis), x)  87.3 us
    another operation x9, other arithmetic, build_element(): factor = jnp.linalg.cholesky(process_info + information)  72.6 us
    another operation x86, local copies, waits for them, and re-layouts, invert_shifted(): return jax.scipy.linalg.cho_solve((factor, True), matrix.T)  54.9 us
    all_to_all x1, blocking collectives, body(): lax.all_to_all(weighted, 'tm', split_axis=0, concat_axis=1, tiled=True)  50.4 us
    another operation x4, other arithmetic, build_element(): jax.scipy.linalg.cho_solve((factor, True), jnp.eye(state_dim, dtype=jnp.f...  43.4 us
  transfers between devices with their start and end apart: 9, of which 7 were waited for; matrix products, arithmetic and copies ran while one was open for 1% of the time, Pallas kernels for 0%

commit v1 on v0

v1 whole, which is shorter than its diff:
```python
import functools

import jax
import jax.numpy as jnp
from jax import lax
from jax.experimental import pallas as pl
from jax.experimental.pallas import tpu as pltpu
from jax.sharding import PartitionSpec as P

highest = lax.Precision.HIGHEST
everyone = ("tm", "sensor", "state")
pad = 8

QUICK_STEPS = 12
SURE_STEPS = 48


def matmul(first_op, second_op):
    return jnp.dot(first_op, second_op, precision=highest)


def full(a, b, ca=1, cb=0):
    return lax.dot_general(
        a, b, (((ca,), (cb,)), ((), ())), precision=highest, preferred_element_type=jnp.float32
    )


def rough(a, b):
    return jnp.dot(
        a.astype(jnp.bfloat16), b.astype(jnp.bfloat16), preferred_element_type=jnp.float32
    )


def identity(n):
    return lax.broadcasted_iota(jnp.int32, (n, n), 0) == lax.broadcasted_iota(
        jnp.int32, (n, n), 1
    )


def invert(matrix, scaled_ref, x_ref):
    n = matrix.shape[0]
    eye = identity(n)
    unit = jnp.where(eye, 1.0, 0.0)
    kept = jnp.where(eye, matrix, 0.0)
    along = lax.rsqrt(jnp.sum(kept, axis=0, keepdims=True))
    down = lax.rsqrt(jnp.sum(kept, axis=1, keepdims=True))
    scaled = matrix * down * along
    scaled_ref[...] = scaled
    alpha = n / jnp.sum(scaled * scaled)
    x_ref[...] = (2.0 * alpha) * unit - (alpha * alpha) * scaled

    def quick(carry):
        count, unused = carry
        x = x_ref[...]
        rest = unit - rough(scaled_ref[...], x)
        size = jnp.sum(rest * rest)
        x_ref[...] = x + rough(x, rest)
        return (count + 1, size)

    unused, size = lax.while_loop(
        lambda c: (c[0] < QUICK_STEPS) & (c[1] > 0.25), quick, (0, jnp.float32(1e3))
    )

    @pl.when(jnp.logical_not(size <= 0.25))
    def _():
        rows = jnp.sum(jnp.abs(scaled_ref[...]), axis=0, keepdims=True)
        x_ref[...] = unit / jnp.max(rows)

    def sure(carry):
        count, unused = carry
        x = x_ref[...]
        rest = unit - full(scaled_ref[...], x)
        size = jnp.sum(rest * rest)
        x_ref[...] = x + full(x, rest + rough(rest, rest))
        return (count + 1, size)

    lax.while_loop(lambda c: (c[0] < SURE_STEPS) & (c[1] > 3e-4), sure, (0, jnp.float32(1e3)))
    return x_ref[...] * down * along


def combine_kernel(flag_ref, a_ref, b_ref, out_ref, scaled_ref, x_ref):
    n = b_ref.shape[1]

    @pl.when(flag_ref[0] == 0)
    def _():
        out_ref[...] = b_ref[...]

    @pl.when(flag_ref[0] != 0)
    def _():
        inverse = invert(a_ref[2 * n : 3 * n] + b_ref[0:n], scaled_ref, x_ref)
        x_ref[...] = inverse
        left = a_ref[n : 2 * n]
        right = b_ref[n : 2 * n]
        left_x = full(left, x_ref[...])
        x_right = full(x_ref[...], right)
        mid = a_ref[3 * n + 1 : 3 * n + 2] + b_ref[3 * n : 3 * n + 1]
        mid = jnp.broadcast_to(mid, (pad, n))
        out_ref[0:n] = a_ref[0:n] - full(left_x, left, 1, 1)
        out_ref[n : 2 * n] = -full(left_x, right)
        out_ref[2 * n : 3 * n] = b_ref[2 * n : 3 * n] - full(right, x_right, 0, 0)
        row = lax.broadcasted_iota(jnp.int32, (pad, n), 0)
        first = a_ref[3 * n : 3 * n + 1] - full(mid, left_x, 1, 1)
        second = b_ref[3 * n + 1 : 3 * n + 2] - full(mid, x_right)
        out_ref[3 * n : 3 * n + pad] = jnp.where(
            row == 0, first, jnp.where(row == 1, second, 0.0)
        )


def advance_into(flag_ref, a_ref, b_ref, out_ref, scaled_ref, x_ref):
    n = b_ref.shape[1]

    @pl.when(flag_ref[0] == 0)
    def _():
        out_ref[...] = b_ref[2 * n : 3 * n + pad]

    @pl.when(flag_ref[0] != 0)
    def _():
        inverse = invert(a_ref[0:n] + b_ref[0:n], scaled_ref, x_ref)
        right = b_ref[n : 2 * n]
        x_right = full(inverse, right)
        mid = a_ref[n + 1 : n + 2] + b_ref[3 * n : 3 * n + 1]
        mid = jnp.broadcast_to(mid, (pad, n))
        out_ref[0:n] = b_ref[2 * n : 3 * n] - full(right, x_right, 0, 0)
        second = b_ref[3 * n + 1 : 3 * n + 2] - full(mid, x_right)
        row = lax.broadcasted_iota(jnp.int32, (pad, n), 0)
        out_ref[n : n + pad] = jnp.where(row == 1, second, 0.0)


def advance_kernel(flag_ref, a_ref, b_ref, out_ref, scaled_ref, x_ref):
    advance_into(flag_ref, a_ref, b_ref, out_ref, scaled_ref, x_ref)


def moments(s_ref, cov_ref, mean_ref, scaled_ref, x_ref):
    n = s_ref.shape[1]
    cov = invert(s_ref[0:n], scaled_ref, x_ref)
    cov_ref[...] = cov
    mean_ref[...] = full(s_ref[n : n + pad], cov, 1, 1)


def moments_kernel(s_ref, cov_ref, mean_ref, scaled_ref, x_ref):
    moments(s_ref, cov_ref, mean_ref, scaled_ref, x_ref)


def last_kernel(flag_ref, a_ref, b_ref, cov_ref, mean_ref, s_ref, scaled_ref, x_ref):
    advance_into(flag_ref, a_ref, b_ref, s_ref, scaled_ref, x_ref)
    moments(s_ref, cov_ref, mean_ref, scaled_ref, x_ref)


vmem = pl.BlockSpec(memory_space=pltpu.VMEM)
smem = pl.BlockSpec(memory_space=pltpu.SMEM)


def call(kernel, specs, shapes, n, *extra):
    return pl.pallas_call(
        kernel,
        out_shape=shapes,
        in_specs=specs,
        out_specs=jax.tree.map(lambda unused: vmem, shapes),
        scratch_shapes=[*extra, pltpu.VMEM((n, n), jnp.float32), pltpu.VMEM((n, n), jnp.float32)],
        compiler_params=pltpu.CompilerParams(vmem_limit_bytes=40 * 1024 * 1024),
        cost_estimate=pl.CostEstimate(flops=20_000_000_000, bytes_accessed=3_000_000, transcendentals=0),
    )


def f32(*shape):
    return jax.ShapeDtypeStruct(shape, jnp.float32)


def combine(flag, earlier, later):
    n = later.shape[1]
    return call(combine_kernel, [smem, vmem, vmem], f32(3 * n + pad, n), n)(flag, earlier, later)


def advance(flag, earlier, later):
    n = later.shape[1]
    return call(advance_kernel, [smem, vmem, vmem], f32(n + pad, n), n)(flag, earlier, later)


def filtered(state):
    n = state.shape[1]
    return call(moments_kernel, [vmem], (f32(n, n), f32(pad, n)), n)(state)


def filtered_after(flag, earlier, later):
    n = later.shape[1]
    return call(
        last_kernel,
        [smem, vmem, vmem],
        (f32(n, n), f32(pad, n)),
        n,
        pltpu.VMEM((n + pad, n), jnp.float32),
    )(flag, earlier, later)


def gram_terms(weighted, signal):
    gram_part = jnp.einsum("tms,tmu->tsu", weighted, weighted, preferred_element_type=jnp.float32)
    info_part = jnp.einsum("tm,tms->ts", signal, weighted, preferred_element_type=jnp.float32)
    return (gram_part, info_part)


def shift_right(x, peers, shift):
    return lax.ppermute(x, everyone, [(k, k + shift) for k in range(peers - shift)])


def body(obs_rows, readings, available, sensor_ids, noise_var, col_scale, transition, process_info):
    n = obs_rows.shape[2]
    sensor_total = noise_var.shape[0]
    lookup_table = (
        sensor_ids[:, None] == jnp.arange(sensor_total, dtype=jnp.int32)[None, :]
    ).astype(jnp.float32)
    local_var = matmul(lookup_table, noise_var)
    weight = available.astype(jnp.float32) * lax.rsqrt(local_var)[None, :]
    weighted = (obs_rows.astype(jnp.float32) * weight[:, :, None]).astype(jnp.bfloat16)
    signal = (readings * weight).astype(jnp.bfloat16)
    arrived = (
        lax.all_to_all(weighted, "tm", split_axis=0, concat_axis=1, tiled=True),
        lax.all_to_all(signal, "tm", split_axis=0, concat_axis=1, tiled=True),
    )
    gram_part, info_part = gram_terms(arrived[0], arrived[1])
    gram_part, info_part = (
        lax.psum_scatter(gram_part, ("sensor", "state"), scatter_dimension=0, tiled=True),
        lax.psum_scatter(info_part, ("sensor", "state"), scatter_dimension=0, tiled=True),
    )
    block_len = gram_part.shape[0]
    peers, mine = lax.axis_size(everyone), lax.axis_index(everyone)
    carried = matmul(process_info, transition)
    inward = matmul(transition.T, carried)
    outer_scale = col_scale[:, None] * col_scale[None, :]

    def element(k):
        keep = (mine * block_len + k > 0).astype(jnp.float32)
        vectors = jnp.concatenate(
            [
                jnp.zeros((1, n), jnp.float32),
                (info_part[k] * col_scale)[None, :],
                jnp.zeros((pad - 2, n), jnp.float32),
            ]
        )
        return jnp.concatenate(
            [
                inward * keep,
                carried.T * -keep,
                process_info + gram_part[k] * outer_scale,
                vectors,
            ]
        )

    elements = [element(k) for k in range(block_len)]
    always = jnp.ones((1,), jnp.int32)
    summary = elements[0]
    for k in range(1, block_len):
        summary = combine(always, summary, elements[k])

    shift = 1
    while 2 * shift < peers:
        summary = combine((mine >= shift).astype(jnp.int32)[None], shift_right(summary, peers, shift), summary)
        shift *= 2
    before = shift_right(summary[2 * n :], peers, shift)
    state = advance((mine >= shift).astype(jnp.int32)[None], before, summary)

    before = shift_right(state, peers, 1)
    covs, means = [], []
    later = (mine > 0).astype(jnp.int32)[None]
    cov_end, mean_end = filtered(state)
    for k in range(block_len - 1):
        cov, mean = filtered_after(later, before, elements[k])
        if k < block_len - 2:
            before = advance(later, before, elements[k])
            later = always
        covs.append(cov)
        means.append(mean[1])
    covs.append(cov_end)
    means.append(mean_end[1])
    return (jnp.stack(means), jnp.stack(covs))


def solution(mesh):
    in_specs = (
        P("groups", ("tm", "sensor", "state"), None),
        P("groups", ("tm", "sensor", "state")),
        P("groups", ("tm", "sensor", "state")),
        P(("groups", "tm", "sensor", "state")),
        P(),
        P(),
        P(),
        P(),
    )
    out_specs = (
        P(("groups", "tm", "sensor", "state"), None),
        P(("groups", "tm", "sensor", "state"), None, None),
    )
    return jax.shard_map(body, mesh=mesh, in_specs=in_specs, out_specs=out_specs, check_vma=False)
```

time: 1350 us -> 215 us (0.16)
  other arithmetic: 842 us -> 5.88 us
  matrix products: 145 us -> 5.8 us
  waiting for transfers between devices: 150 us -> 69.9 us
  local copies, waits for them, and re-layouts: 76.5 us -> 1.9 us
  Pallas kernels: 0 us -> 33.4 us
  blocking collectives: 82.3 us -> 57.5 us
  starting transfers between devices: 4.83 us -> 24.2 us
  loops' own time: 14.2 us -> 0 us
    another operation x140 -> x2, other arithmetic: 832 us -> 1.43 us  [body(): return (jnp.stack(means), jnp.stack(covs))]
    dot_general x137 -> x3, matrix products: 98.1 us -> 3.29 us  [matmul(): return jnp.dot(first_op, second_op, precision=highest)]
    all_gather x6 -> x0, waiting for transfers between devices: 87.3 us -> none  [prefix(): everything = jax.tree.map(lambda part: lax.all_gather(part, axis), x)]
    another operation x127 -> x2, local copies, waits for them, and re-layouts: 62 us -> 0.01 us  [the longest x86 54.9 us: invert_shifted(): return jax.scipy.linalg.cho_solve((factor, True), matrix.T)]
    ppermute x0 -> x5, waiting for transfers between devices: none -> 52.3 us  [shift_right(): lax.ppermute(x, everyone, [(k, k + shift) for k in range(peers - shift)])]
    another operation x112 -> x0, matrix products: 44.5 us -> none  [the longest x78 27.3 us: invert_shifted(): return jax.scipy.linalg.cho_solve((factor, True), matrix.T)]
    psum x1 -> x0, waiting for transfers between devices: 33.6 us -> none  [from_root(): return lax.psum(jnp.where(mine, x, jnp.zeros_like(x)), axis)]
    pallas_call x0 -> x7, Pallas kernels: none -> 33.4 us  [the longest x4 16.2 us: combine(): call(combine_kernel, [smem, vmem, vmem], f32(3 * n + pad, n), n)]
  transfers between devices with their start and end apart: 9 -> 7, of which waited for: 7 -> 5; matrix products, arithmetic and copies ran while one was open for 1% -> 1% of each run, Pallas kernels for 0% -> 2%
where the time goes in v1:
time: 215 us; the launch traced here: 213 us
  waiting for transfers between devices  69.9 us (33%)
  blocking collectives  57.5 us (27%)
  Pallas kernels  33.4 us (16%)
  starting transfers between devices  24.2 us (11%)
  between operations  14.9 us (7%)
  other arithmetic  5.88 us (3%)
  matrix products  5.8 us (3%)
    ppermute x5, waiting for transfers between devices, shift_right(): lax.ppermute(x, everyone, [(k, k + shift) for k in range(peers - shift)])  52.3 us
    all_to_all x1, blocking collectives, body(): lax.all_to_all(weighted, 'tm', split_axis=0, concat_axis=1, tiled=True)  50.4 us
    ppermute x5, starting transfers between devices, shift_right(): lax.ppermute(x, everyone, [(k, k + shift) for k in range(peers - shift)])  19.5 us
    reduce_scatter x1, waiting for transfers between devices, body(): lax.psum_scatter(gram_part, ('sensor', 'state'), scatter_dimension=0, til...  17.6 us
    pallas_call x4, Pallas kernels, combine(): call(combine_kernel, [smem, vmem, vmem], f32(3 * n + pad, n), n)  16.2 us
    pallas_call x1, Pallas kernels, filtered_after(): call(last_kernel, [smem, vmem, vmem], (f32(n, n), f32(pad, n)), n, pltpu....  8.39 us
    unnamed x1, blocking collectives  7.13 us
    pallas_call x1, Pallas kernels, advance(): call(advance_kernel, [smem, vmem, vmem], f32(n + pad, n), n)  4.75 us
  transfers between devices with their start and end apart: 7, of which 5 were waited for; matrix products, arithmetic and copies ran while one was open for 1% of the time, Pallas kernels for 2%

profile of v1, /device:TPU:29, one launch (start us, length us, event | category | flops | bytes accessed | tf_op | source)
XLA Modules:
  0.0 213.5 jit_solution(4418920703984924615)
XLA Ops:
  7.2 0.0 copy-start
  7.2 0.0 reduce-scatter.2.cloned.1.call-start
  7.2 1.4 fusion
  8.6 1.4 fusion.6
  10.0 1.9 multiply_convert_fusion
  11.9 50.4 %all_to_all.37 = bf16[32,128,256]{2,1,0:T(8,128)(2,1)S(1)} all-to-all(bf16[32,128,256]{2,1,0:T(8,128)(2,1)S(1)} %multiply_convert_fusion), channel_id=1, replica_groups=mesh['groups'=2,'tm'=4,'sensor'=2,'state'=2] {'tm'}, dimensions={0} | all-to-all | bytes 4194304 | tf_op jit(solution)/shard_map/all_to_all | solution.py:216
  62.3 0.1 copy.12
  62.4 2.1 fusion.9
  64.6 0.0 copy-start.1
  64.6 0.0 copy-start.3
  64.6 0.0 reduce-scatter.2.cloned.1.call-update
  64.6 4.7 %all-to-all-start.1 = ((bf16[4,8,128]{2,1,0:T(8,128)(2,1)}), bf16[4,8,128]{2,1,0:T(8,128)(2,1)S(1)}, u32[]{:S(2)}, u32[]{:S(2)}) async-start(bf16[4,8,128]{2,1,0:T(8,128)(2,1)} %get-tuple-element.10), calls=%async_computation.2 | async-start | bytes 16384 | tf_op jit(solution)/shard_map/all_to_all | solution.py:217
  69.3 0.0 copy-done
  69.3 0.0 copy-done.1
  69.3 0.0 copy-start.2
  69.3 0.6 fusion.8
  69.9 1.3 multiply_bitcast_fusion
  71.2 0.0 copy-done.3
  71.2 0.6 dynamic-slice
  72.4 0.0 all-to-all-done.1
  72.4 0.4 fusion.4
  72.8 7.1 %all-reduce = f32[8,256]{1,0:T(8,128)S(1)} all-reduce(f32[8,256]{1,0:T(8,128)S(1)} %bitcast.61), channel_id=3, replica_groups=mesh['groups'=2,'tm'=4,'sensor'=2,'state'=2] {'sensor','state'}, use_global_device_ids=true, to_apply=%region_1.0.clone | all-reduce | flops 2048 | bytes 16384
  80.0 0.0 copy-done.2
  80.0 17.6 %reduce-scatter.2.cloned.1.call-done = f32[2,256,256]{2,1,0:T(8,128)} async-done(((f32[8,256,256]{2,1,0:T(8,128)}), f32[2,256,256]{2,1,0:T(8,128)}) %reduce-scatter.2.cloned.1.call-update) | async-done | bytes 524304 | tf_op jit(solution)/shard_map/reduce_scatter | solution.py:221
  97.6 1.1 fusion.3
  98.7 1.0 concatenate.6.a_ref.b_ref
  99.8 0.1 concatenate.7.b_ref
  99.8 3.7 %shard_map.95.b_ref = f32[776,256]{1,0:T(8,128)S(1)} custom-call(s32[1]{0:T(128)} %constant.24.clone.1.flag_ref, f32[776,256]{1,0:T(8,128)S(1)} %concatenate.6.a_ref.b_ref, f32[776,256]{1,0:T(8,128)S(1)} %concatenate.7.b_ref), custom_call_target="tpu_custom_call" | custom-call | flops 20000000000 | bytes 3000000 | tf_op jit(solution)/shard_map/pallas_call | solution.py:171
  103.5 2.7 %collective-permute-start = (f32[776,256]{1,0:T(8,128)S(1)}, f32[776,256]{1,0:T(8,128)S(1)}, u32[]{:S(2)}, u32[]{:S(2)}) collective-permute-start(f32[776,256]{1,0:T(8,128)S(1)} %shard_map.95.b_ref), channel_id=1, source_target_pairs={{0,1},{1,2},{2,3},{3,4},{4,5},{5,6},{6,7},{7,8},{8,9},{9,10},{10,1... | collective-permute-start | bytes 2383880 | tf_op jit(solution)/shard_map/ppermute | solution.py:202
  106.3 9.0 %collective-permute-done.a_ref = f32[776,256]{1,0:T(8,128)S(1)} collective-permute-done((f32[776,256]{1,0:T(8,128)S(1)}, f32[776,256]{1,0:T(8,128)S(1)}, u32[]{:S(2)}, u32[]{:S(2)}) %collective-permute-start) | collective-permute-done | bytes 794656 | tf_op jit(solution)/shard_map/ppermute | solution.py:202
  115.3 3.7 %shard_map.96.b_ref = f32[776,256]{1,0:T(8,128)S(1)} custom-call(s32[1]{0:T(128)} %bitcast.4.flag_ref, f32[776,256]{1,0:T(8,128)S(1)} %collective-permute-done.a_ref, f32[776,256]{1,0:T(8,128)S(1)} %shard_map.95.b_ref), custom_call_target="tpu_custom_call" | custom-call | flops 20000000000 | bytes 3000000 | tf_op jit(solution)/shard_map/pallas_call | solution.py:171
  119.0 1.9 collective-permute-start.1
  121.0 16.8 %collective-permute-done.1.a_ref = f32[776,256]{1,0:T(8,128)S(1)} collective-permute-done((f32[776,256]{1,0:T(8,128)S(1)}, f32[776,256]{1,0:T(8,128)S(1)}, u32[]{:S(2)}, u32[]{:S(2)}) %collective-permute-start.1) | collective-permute-done | bytes 794656 | tf_op jit(solution)/shard_map/ppermute | solution.py:202
  137.8 3.8 %shard_map.97.b_ref = f32[776,256]{1,0:T(8,128)S(1)} custom-call(s32[1]{0:T(128)} %bitcast.3.flag_ref, f32[776,256]{1,0:T(8,128)S(1)} %collective-permute-done.1.a_ref, f32[776,256]{1,0:T(8,128)S(1)} %shard_map.96.b_ref), custom_call_target="tpu_custom_call" | custom-call | flops 20000000000 | bytes 3000000 | tf_op jit(solution)/shard_map/pallas_call | solution.py:171
  141.6 1.3 collective-permute-start.2
  142.9 16.1 %collective-permute-done.2.a_ref = f32[776,256]{1,0:T(8,128)S(1)} collective-permute-done((f32[776,256]{1,0:T(8,128)S(1)}, f32[776,256]{1,0:T(8,128)S(1)}, u32[]{:S(2)}, u32[]{:S(2)}) %collective-permute-start.2) | collective-permute-done | bytes 794656 | tf_op jit(solution)/shard_map/ppermute | solution.py:202
  159.0 5.0 %shard_map.98.b_ref = f32[776,256]{1,0:T(8,128)S(1)} custom-call(s32[1]{0:T(128)} %bitcast.2.flag_ref, f32[776,256]{1,0:T(8,128)S(1)} %collective-permute-done.2.a_ref, f32[776,256]{1,0:T(8,128)S(1)} %shard_map.97.b_ref), custom_call_target="tpu_custom_call" | custom-call | flops 20000000000 | bytes 3000000 | tf_op jit(solution)/shard_map/pallas_call | solution.py:171
  164.1 1.3 collective-permute-start.3
  165.4 10.3 %collective-permute-done.3.a_ref = f32[264,256]{1,0:T(8,128)S(1)} collective-permute-done((f32[264,256]{1,0:T(8,128)S(1)}, f32[264,256]{1,0:T(8,128)S(1)}, u32[]{:S(2)}, u32[]{:S(2)}) %collective-permute-start.3) | collective-permute-done | bytes 270368 | tf_op jit(solution)/shard_map/ppermute | solution.py:202
  175.7 4.8 %shard_map.99.s_ref = f32[264,256]{1,0:T(8,128)S(1)} custom-call(s32[1]{0:T(128)} %bitcast.1.flag_ref, f32[264,256]{1,0:T(8,128)S(1)} %collective-permute-done.3.a_ref, f32[776,256]{1,0:T(8,128)S(1)} %shard_map.98.b_ref), custom_call_target="tpu_custom_call" | custom-call | flops 20000000000 | bytes 3000000 | tf_op jit(solution)/shard_map/pallas_call | solution.py:176
  180.5 12.3 %collective-permute-start.4 = (f32[264,256]{1,0:T(8,128)S(1)}, f32[264,256]{1,0:T(8,128)S(1)}, u32[]{:S(2)}, u32[]{:S(2)}) collective-permute-start(f32[264,256]{1,0:T(8,128)S(1)} %shard_map.99.s_ref), channel_id=1, source_target_pairs={{0,1},{1,2},{2,3},{3,4},{4,5},{5,6},{6,7},{7,8},{8,9},{9,10},{10,1... | collective-permute-start | bytes 811016 | tf_op jit(solution)/shard_map/ppermute | solution.py:202
  192.8 4.0 %shard_map.101 = (f32[256,256]{1,0:T(8,128)S(1)}, f32[8,256]{1,0:T(8,128)S(1)}) custom-call(f32[264,256]{1,0:T(8,128)S(1)} %shard_map.99.s_ref), custom_call_target="tpu_custom_call" | custom-call | flops 20000000000 | bytes 3000000 | tf_op jit(solution)/shard_map/pallas_call | solution.py:181
  196.8 0.0 collective-permute-done.4.a_ref
  196.8 8.4 %shard_map.100 = (f32[256,256]{1,0:T(8,128)S(1)}, f32[8,256]{1,0:T(8,128)S(1)}) custom-call(s32[1]{0:T(128)} %bitcast.flag_ref, f32[264,256]{1,0:T(8,128)S(1)} %collective-permute-done.4.a_ref, f32[776,256]{1,0:T(8,128)S(1)} %concatenate.6.a_ref.b_ref), custom_call_target="tpu_custom_call" | custom-call | flops 20000000000 | bytes 3000000 | tf_op jit(solution)/shard_map/pallas_call | solution.py:186
  205.2 0.8 pad_maximum_fusion
  206.0 0.6 pad_maximum_fusion.1
  (8 shorter events, 0.1 us)
Async XLA Ops:
  7.2 62.1 %copy-start = (f32[256,256]{1,0:T(8,128)S(1)}, f32[256,256]{1,0:T(8,128)}, u32[]{:S(2)}) copy-start(f32[256,256]{1,0:T(8,128)} %param.14) | copy-start | bytes 786436
  7.2 90.4 %reduce-scatter.2.cloned.1.call-start = ((), (), s32[]{:S(2)}) async-start(), calls=%async_computation.3 | async-start | bytes 2621440 | tf_op jit(solution)/shard_map/reduce_scatter | solution.py:221
  64.6 4.7 %copy-start.1 = (f32[256,256]{1,0:T(8,128)S(1)}, f32[256,256]{1,0:T(8,128)}, u32[]{:S(2)}) copy-start(f32[256,256]{1,0:T(8,128)} %param.15) | copy-start | bytes 786436
  64.6 6.6 %copy-start.3 = (u32[32]{0:T(128)S(1)}, u32[32]{0:T(128)}, u32[]{:S(2)}) copy-start(u32[32]{0:T(128)} %constant.28) | copy-start | bytes 388
  64.6 7.8 %all-to-all-start.1 = ((bf16[4,8,128]{2,1,0:T(8,128)(2,1)}), bf16[4,8,128]{2,1,0:T(8,128)(2,1)S(1)}, u32[]{:S(2)}, u32[]{:S(2)}) async-start(bf16[4,8,128]{2,1,0:T(8,128)(2,1)} %get-tuple-element.10), calls=%async_computation.2 | async-start | bytes 16384 | tf_op jit(solution)/shard_map/all_to_all | solution.py:217
  69.3 10.7 %copy-start.2 = (f32[256]{0:T(256)S(1)}, f32[256]{0:T(256)}, u32[]{:S(2)}) copy-start(f32[256]{0:T(256)} %param.13) | copy-start | bytes 3076
  103.5 11.8 %collective-permute-start = (f32[776,256]{1,0:T(8,128)S(1)}, f32[776,256]{1,0:T(8,128)S(1)}, u32[]{:S(2)}, u32[]{:S(2)}) collective-permute-start(f32[776,256]{1,0:T(8,128)S(1)} %shard_map.95.b_ref), channel_id=1, source_target_pairs={{0,1},{1,2},{2,3},{3,4},{4,5},{5,6},{6,7},{7,8},{8,9},{9,10},{10,1... | collective-permute-start | bytes 2383880 | tf_op jit(solution)/shard_map/ppermute | solution.py:202
  119.0 18.8 %collective-permute-start.1 = (f32[776,256]{1,0:T(8,128)S(1)}, f32[776,256]{1,0:T(8,128)S(1)}, u32[]{:S(2)}, u32[]{:S(2)}) collective-permute-start(f32[776,256]{1,0:T(8,128)S(1)} %shard_map.96.b_ref), channel_id=1, source_target_pairs={{0,2},{1,3},{2,4},{3,5},{4,6},{5,7},{6,8},{7,9},{8,10},{9,11},{10,... | collective-permute-start | bytes 2383880 | tf_op jit(solution)/shard_map/ppermute | solution.py:202
  141.6 17.4 %collective-permute-start.2 = (f32[776,256]{1,0:T(8,128)S(1)}, f32[776,256]{1,0:T(8,128)S(1)}, u32[]{:S(2)}, u32[]{:S(2)}) collective-permute-start(f32[776,256]{1,0:T(8,128)S(1)} %shard_map.97.b_ref), channel_id=1, source_target_pairs={{0,4},{1,5},{2,6},{3,7},{4,8},{5,9},{6,10},{7,11},{8,12},{9,13},{1... | collective-permute-start | bytes 2383880 | tf_op jit(solution)/shard_map/ppermute | solution.py:202
  164.1 11.6 %collective-permute-start.3 = (f32[264,256]{1,0:T(8,128)S(1)}, f32[264,256]{1,0:T(8,128)S(1)}, u32[]{:S(2)}, u32[]{:S(2)}) collective-permute-start(f32[264,256]{1,0:T(8,128)S(1)} %slice.30), channel_id=1, source_target_pairs={{0,8},{1,9},{2,10},{3,11},{4,12},{5,13},{6,14},{7,15},{16,24},{17,... | collective-permute-start | bytes 811016 | tf_op jit(solution)/shard_map/ppermute | solution.py:202
  180.5 16.3 %collective-permute-start.4 = (f32[264,256]{1,0:T(8,128)S(1)}, f32[264,256]{1,0:T(8,128)S(1)}, u32[]{:S(2)}, u32[]{:S(2)}) collective-permute-start(f32[264,256]{1,0:T(8,128)S(1)} %shard_map.99.s_ref), channel_id=1, source_target_pairs={{0,1},{1,2},{2,3},{3,4},{4,5},{5,6},{6,7},{7,8},{8,9},{9,10},{10,1... | collective-permute-start | bytes 811016 | tf_op jit(solution)/shard_map/ppermute | solution.py:202
Sparse Core Ops, SparseCore 0:
  64.7 32.8 reduce-scatter.1
